TPU v7x, 32 devices: a whole 2x2x4 slice. The times are simulated.
32 devices in a mesh: ens: 2 (over y), lon: 4 (over z), lat: 4 (over x, core).
Axes of the slice: x: 2, y: 2, z: 4, core: 2. Of those that a mesh axis runs over, the one named last changes fastest.
Arguments:
- bed_depth: float32 [256, 4096], P('lat', 'lon'), may hold values from 0.5 to 2
- cotangent: float32 [512, 4096], P(('ens', 'lat'), 'lon'), parts along dimension 0, may hold values from -6 to 6
- sample_cell: int32 [131072], P(('lon', 'lat')), may hold values from 0 to 65535
- sample_owner: int32 [131072], P(('lon', 'lat')), may hold values from 0 to 15, as said below
- sample_reach: int32 [131072], P(('lon', 'lat')), may hold values from 0 to 1023
- sample_weight: float32 [131072], P(('lon', 'lat')), may hold values from 0.05 to 0.5
- sample_angle: float32 [131072], P(('lon', 'lat')), may hold values from -3.140625 to 3.140625
- sample_count: int32 [16], P(('lon', 'lat')), may hold values from 768 to 8192, as said below
- reach_width: float32 [16384], P(('lon', 'lat')), may hold values from 0.5 to 4
- reach_bed: float32 [16384], P(('lon', 'lat')), may hold values from 0.5 to 3
Outputs:
- grad_level: float32 [512, 4096], P(('ens', 'lat'), 'lon'), parts along dimension 0
- grad_width: float32 [32768], P(('ens', 'lon', 'lat')), parts along dimension 0
- grad_bed: float32 [32768], P(('ens', 'lon', 'lat')), parts along dimension 0
There are 2 independent parts, one for each index of `ens`. A program takes and returns all parts, laid end to end along the dimension named above; an argument that names none is the same for every part. Nothing has to cross between parts.
Inputs may be any that keep to these rules, and one draw needn't show every extreme that they name: `sample_owner`: among the 8192 slots of one device at most 576 name any one owner, and in every draw one owner is named by exactly 576 live slots of every device. Slots 0 to sample_count - 1 of a device are live. Some device has all 8192 slots live.
All inputs are finite; a program needn't handle non-finite values.
Results may differ from a plain program's by a relative error of at most 0.0003.
Values sent between devices are 32-bit elements; how exact they have to be, the bound alone decides.
A program may use at most 192 MiB of HBM per device.

v0:
```python
import math

import jax
import jax.numpy as jnp
from jax import lax
from jax.sharding import PartitionSpec as P

STEPS = 4


WAVE_GAIN = 0.2
DRAG_RATE = 0.05
EXACT = lax.Precision.HIGHEST


def padded(value, sides, width, wrap):
    for axis, dim in sides:
        devices, length = (lax.axis_size(axis), value.shape[dim])
        up = [(i, (i + 1) % devices) for i in range(devices if wrap else devices - 1)]
        down = [(j, i) for i, j in up]
        last = lax.slice_in_dim(value, length - width, length, axis=dim)
        leading = lax.slice_in_dim(value, 0, width, axis=dim)
        before = lax.ppermute(last, axis, up)
        after = lax.ppermute(leading, axis, down)
        value = jnp.concatenate([before, value, after], axis=dim)
    return value


def extend(stacked, margin):
    taller = padded(stacked, (("lat", 1),), margin, False)
    return padded(taller, (("lon", 2),), margin, True)


def coefficients(bed_field, north_ok):
    east_depth = 0.5 * (bed_field + jnp.concatenate([bed_field[:, 1:], bed_field[:, -1:]], axis=1))
    north_depth = 0.5 * (bed_field + jnp.concatenate([bed_field[1:], bed_field[-1:]], axis=0))
    east_keep = 1.0 / (1.0 + DRAG_RATE / east_depth)
    north_keep = jnp.where(north_ok, 1.0 / (1.0 + DRAG_RATE / north_depth), 0.0)
    return (
        east_keep,
        WAVE_GAIN * east_keep * east_depth,
        north_keep,
        WAVE_GAIN * north_keep * north_depth,
    )


def back_step(widened, coefs, north_ok, offset):
    level_adj, east_adj, north_adj = (widened[0], widened[1], widened[2])
    span_rows, span_cols = level_adj.shape
    east_keep, east_gain, north_keep, north_gain = coefs
    east_mid = east_adj[1:-1, :-1] + level_adj[1:-1, 1:] - level_adj[1:-1, :-1]
    row_select = north_ok[offset : offset + span_rows - 1, offset + 1 : offset + span_cols - 1]
    north_mid = jnp.where(
        row_select, north_adj[:-1, 1:-1] + level_adj[1:, 1:-1] - level_adj[:-1, 1:-1], 0.0
    )
    east_flux = (
        east_gain[offset + 1 : offset + span_rows - 1, offset : offset + span_cols - 1] * east_mid
    )
    north_flux = (
        north_gain[offset : offset + span_rows - 1, offset + 1 : offset + span_cols - 1] * north_mid
    )
    new_level = (
        level_adj[1:-1, 1:-1]
        + east_flux[:, 1:]
        - east_flux[:, :-1]
        + north_flux[1:]
        - north_flux[:-1]
    )
    inner_rows = slice(offset + 1, offset + span_rows - 1)
    inner_cols = slice(offset + 1, offset + span_cols - 1)
    new_east = east_keep[inner_rows, inner_cols] * east_mid[:, 1:]
    new_north = north_keep[inner_rows, inner_cols] * north_mid[1:]
    return (jnp.stack([new_level, new_east, new_north]), east_mid[:, 1:], north_mid[1:])


def sample_values(fields, cells, core_cols):
    slot_total = cells.shape[0]
    block = math.gcd(slot_total, 512)
    row_ids = jnp.arange(fields.shape[1])
    col_ids = jnp.arange(core_cols)
    cell_rows = (cells // core_cols).reshape(-1, block)
    cell_cols = (cells % core_cols).reshape(-1, block)

    def one_block(pair):
        rows_here, cols_here = pair
        row_hot = (rows_here[:, None] == row_ids[None, :]).astype(jnp.float32)
        picked = jnp.einsum("sr,frc->fsc", row_hot, fields, precision=EXACT)
        col_hot = (cols_here[:, None] == col_ids[None, :])[None]
        return jnp.sum(jnp.where(col_hot, picked, 0.0), axis=2)

    values = lax.map(one_block, (cell_rows, cell_cols))
    return jnp.transpose(values, (1, 0, 2)).reshape(fields.shape[0], slot_total)


def on_device(
    bed_depth,
    cotangent,
    sample_cell,
    sample_owner,
    sample_reach,
    sample_weight,
    sample_angle,
    sample_count,
    reach_width,
    reach_bed,
):
    core_rows, core_cols = bed_depth.shape
    grid_rows = core_rows * lax.axis_size("lat")
    blank = jnp.zeros_like(cotangent)
    stacked = jnp.stack([cotangent, blank, blank])
    depth = 1
    bed_wide = extend(bed_depth[None], depth)[0]
    row_global = lax.axis_index("lat") * core_rows - depth + jnp.arange(core_rows + 2 * depth)
    inside = (row_global >= 0) & (row_global < grid_rows)
    north_row = (row_global >= 0) & (row_global < grid_rows - 1)
    north_ok = jnp.broadcast_to(north_row[:, None], (core_rows + 2 * depth, core_cols + 2 * depth))
    bed_wide = jnp.where(inside[:, None], bed_wide, 1.0)
    coefs = coefficients(bed_wide, north_ok)
    sum_level = blank
    sum_east = blank
    sum_north = blank
    for group_index in range(STEPS // depth):
        widened = extend(stacked, depth)
        sum_level = sum_level + widened[0, 1 : 1 + core_rows, 1 : 1 + core_cols]
        widened, east_mid, north_mid = back_step(widened, coefs, north_ok, depth - 1)
        sum_east = sum_east + east_mid
        sum_north = sum_north + north_mid
        stacked = widened
    slot_total = sample_cell.shape[0]
    live_slot = jnp.arange(slot_total) < sample_count[0]
    picked = sample_values(jnp.stack([sum_level, sum_east, sum_north]), sample_cell, core_cols)
    level_term = jnp.where(live_slot, sample_weight * picked[0], 0.0)
    flow_term = jnp.where(
        live_slot,
        sample_weight * (jnp.cos(sample_angle) * picked[1] + jnp.sin(sample_angle) * picked[2]),
        0.0,
    )
    owners = lax.axis_size(("lon", "lat"))
    reach_count = reach_width.shape[0]
    owner_ids = jnp.arange(owners)
    reach_ids = jnp.arange(reach_count)
    block = math.gcd(slot_total, 512)
    block_count = slot_total // block
    owner_blocks = sample_owner.reshape(block_count, block)
    reach_blocks = sample_reach.reshape(block_count, block)
    term_blocks = jnp.transpose(
        jnp.stack([level_term, flow_term]).reshape(2, block_count, block), (1, 0, 2)
    )

    def add_block(total, pack):
        owner_here, reach_here, terms_here = pack
        owner_hot = (owner_here[:, None] == owner_ids[None, :]).astype(jnp.float32)
        reach_hot = (reach_here[:, None] == reach_ids[None, :]).astype(jnp.float32)
        weighted = owner_hot[None] * terms_here[:, :, None]
        return (total + jnp.einsum("tso,sr->tor", weighted, reach_hot, precision=EXACT), None)

    partial_sums, unused = lax.scan(
        add_block,
        jnp.zeros((2, owners, reach_count), jnp.float32),
        (owner_blocks, reach_blocks, term_blocks),
    )
    totals = lax.psum_scatter(
        partial_sums.reshape(2, owners * reach_count),
        ("lon", "lat"),
        scatter_dimension=1,
        tiled=True,
    )
    grad_width = reach_bed * totals[0]
    grad_bed = reach_width * totals[0] + reach_bed * totals[1]
    return (stacked[0], grad_width, grad_bed)


def solution(mesh):
    placed = (
        P("lat", "lon"),
        P(("ens", "lat"), "lon"),
        P(("lon", "lat")),
        P(("lon", "lat")),
        P(("lon", "lat")),
        P(("lon", "lat")),
        P(("lon", "lat")),
        P(("lon", "lat")),
        P(("lon", "lat")),
        P(("lon", "lat")),
    )
    return jax.shard_map(
        on_device,
        mesh=mesh,
        in_specs=placed,
        out_specs=(P(("ens", "lat"), "lon"), P(("ens", "lon", "lat")), P(("ens", "lon", "lat"))),
        check_vma=False,
    )
```

profile of v0, /device:TPU:0, one launch (start us, length us, event | category | flops | bytes accessed | tf_op | source)
XLA Modules:
  0.0 319.2 jit_solution(11375084547940642462)
XLA Ops:
  12.4 5.1 %collective-permute-start = (f32[3,1,1024]{2,1,0:T(1,128)S(1)}, f32[3,1,1024]{2,1,0:T(1,128)S(1)}, u32[]{:S(2)}, u32[]{:S(2)}) collective-permute-start(f32[3,1,1024]{2,1,0:T(1,128)S(1)} %get-tuple-element.196), channel_id=1, source_target_pairs={{0,1},{1,2},{2,3},{4,5},{5,6},{6,7},{8,9},{9,10},{10,11},{12,13},{... | collective-permute-start | bytes 36872 | tf_op jit(solution)/shard_map/ppermute | solution.py:23
  20.0 3.6 %collective-permute-start.7 = (f32[1,66,1]{2,1,0:T(8,128)S(1)}, f32[1,66,1]{2,1,0:T(8,128)S(1)}, u32[]{:S(2)}, u32[]{:S(2)}) collective-permute-start(f32[1,66,1]{2,1,0:T(8,128)S(1)} %get-tuple-element.192), channel_id=1, source_target_pairs={{4,0},{8,4},{12,8},{0,12},{5,1},{9,5},{13,9},{1,13},{6,2},{10,6},{... | collective-permute-start | bytes 800 | tf_op jit(solution)/shard_map/ppermute | solution.py:24
  25.3 4.1 %collective-permute-done.6 = f32[1,66,1]{2,1,0:T(8,128)S(1)} collective-permute-done((f32[1,66,1]{2,1,0:T(8,128)S(1)}, f32[1,66,1]{2,1,0:T(8,128)S(1)}, u32[]{:S(2)}, u32[]{:S(2)}) %collective-permute-start.6) | collective-permute-done | bytes 296 | tf_op jit(solution)/shard_map/ppermute | solution.py:23
  33.2 5.3 %collective-permute-done.3 = f32[3,66,1]{2,1,0:T(8,128)S(1)} collective-permute-done((f32[3,66,1]{2,1,0:T(8,128)S(1)}, f32[3,66,1]{2,1,0:T(8,128)S(1)}, u32[]{:S(2)}, u32[]{:S(2)}) %collective-permute-start.3) | collective-permute-done | bytes 824 | tf_op jit(solution)/shard_map/ppermute | solution.py:24
  45.5 4.0 %collective-permute-done.9 = f32[3,1,1024]{2,1,0:T(1,128)S(1)} collective-permute-done((f32[3,1,1024]{2,1,0:T(1,128)S(1)}, f32[3,1,1024]{2,1,0:T(1,128)S(1)}, u32[]{:S(2)}, u32[]{:S(2)}) %collective-permute-start.9) | collective-permute-done | bytes 12320 | tf_op jit(solution)/shard_map/ppermute | solution.py:24
  51.8 2.7 collective-permute-done.11
  54.5 2.6 collective-permute-done.10
  59.6 3.0 collective-permute-start.12
  68.3 2.7 collective-permute-done.15
  71.0 3.4 %collective-permute-done.14 = f32[3,66,1]{2,1,0:T(8,128)S(1)} collective-permute-done((f32[3,66,1]{2,1,0:T(8,128)S(1)}, f32[3,66,1]{2,1,0:T(8,128)S(1)}, u32[]{:S(2)}, u32[]{:S(2)}) %collective-permute-start.14) | collective-permute-done | bytes 824 | tf_op jit(solution)/shard_map/ppermute | solution.py:23
  79.2 2.6 collective-permute-start.16
  83.2 2.4 collective-permute-done.17
  96.8 76.7 %while.22 = (s32[]{:T(128)}, f32[16,3,512]{2,1,0:T(4,128)S(1)}, s32[16,512]{1,0:T(8,128)}, s32[16,512]{1,0:T(8,128)}, f32[3,64,1024]{2,1,0:T(8,128)S(1)}, /*index=5*/s32[]{:T(128)}) while((s32[]{:T(128)}, f32[16,3,512]{2,1,0:T(4,128)S(1)}, s32[16,512]{1,0:T(8,128)}, s32[16,512]{1,0:T(8,128)}, f32[3,64,1024]{2,1,0:T(8,128)S(1)}, ...), condition=%wide.region_2.3_spmd.clone, body=%wide.region_0.2_spmd.clone.sunk | while | flops 1211660800 | bytes 1869909 | solution.py:91
  98.0 3.6 %select_reduce_fusion.2 = f32[512,3]{0,1:T(4,128)S(1)} fusion(pred[512,1024]{1,0:T(8,128)(4,1)S(1)} %iota_compare_fusion.6, f32[3,64,1024]{2,1,0:T(8,128)S(1)} %get-tuple-element.295, s32[512]{0:T(512)S(1)} %bitcast.127), kind=kOutput, calls=%fused_computation.4.clone.1 | convolution fusion | flops 1211136512 | bytes 1318912 | tf_op jit(solution)/shard_map/while/body/eval_jaxpr/sr,frc->fsc/dot_general | solution.py:87
  102.7 3.7 %select_reduce_fusion.2 = f32[512,3]{0,1:T(4,128)S(1)} fusion(pred[512,1024]{1,0:T(8,128)(4,1)S(1)} %iota_compare_fusion.6, f32[3,64,1024]{2,1,0:T(8,128)S(1)} %get-tuple-element.295, s32[512]{0:T(512)S(1)} %bitcast.127), kind=kOutput, calls=%fused_computation.4.clone.1 | convolution fusion | flops 1211136512 | bytes 1318912 | tf_op jit(solution)/shard_map/while/body/eval_jaxpr/sr,frc->fsc/dot_general | solution.py:87
  107.5 3.6 %select_reduce_fusion.2 = f32[512,3]{0,1:T(4,128)S(1)} fusion(pred[512,1024]{1,0:T(8,128)(4,1)S(1)} %iota_compare_fusion.6, f32[3,64,1024]{2,1,0:T(8,128)S(1)} %get-tuple-element.295, s32[512]{0:T(512)S(1)} %bitcast.127), kind=kOutput, calls=%fused_computation.4.clone.1 | convolution fusion | flops 1211136512 | bytes 1318912 | tf_op jit(solution)/shard_map/while/body/eval_jaxpr/sr,frc->fsc/dot_general | solution.py:87
  112.3 3.7 %select_reduce_fusion.2 = f32[512,3]{0,1:T(4,128)S(1)} fusion(pred[512,1024]{1,0:T(8,128)(4,1)S(1)} %iota_compare_fusion.6, f32[3,64,1024]{2,1,0:T(8,128)S(1)} %get-tuple-element.295, s32[512]{0:T(512)S(1)} %bitcast.127), kind=kOutput, calls=%fused_computation.4.clone.1 | convolution fusion | flops 1211136512 | bytes 1318912 | tf_op jit(solution)/shard_map/while/body/eval_jaxpr/sr,frc->fsc/dot_general | solution.py:87
  117.1 3.6 %select_reduce_fusion.2 = f32[512,3]{0,1:T(4,128)S(1)} fusion(pred[512,1024]{1,0:T(8,128)(4,1)S(1)} %iota_compare_fusion.6, f32[3,64,1024]{2,1,0:T(8,128)S(1)} %get-tuple-element.295, s32[512]{0:T(512)S(1)} %bitcast.127), kind=kOutput, calls=%fused_computation.4.clone.1 | convolution fusion | flops 1211136512 | bytes 1318912 | tf_op jit(solution)/shard_map/while/body/eval_jaxpr/sr,frc->fsc/dot_general | solution.py:87
  121.9 3.7 %select_reduce_fusion.2 = f32[512,3]{0,1:T(4,128)S(1)} fusion(pred[512,1024]{1,0:T(8,128)(4,1)S(1)} %iota_compare_fusion.6, f32[3,64,1024]{2,1,0:T(8,128)S(1)} %get-tuple-element.295, s32[512]{0:T(512)S(1)} %bitcast.127), kind=kOutput, calls=%fused_computation.4.clone.1 | convolution fusion | flops 1211136512 | bytes 1318912 | tf_op jit(solution)/shard_map/while/body/eval_jaxpr/sr,frc->fsc/dot_general | solution.py:87
  126.7 3.6 %select_reduce_fusion.2 = f32[512,3]{0,1:T(4,128)S(1)} fusion(pred[512,1024]{1,0:T(8,128)(4,1)S(1)} %iota_compare_fusion.6, f32[3,64,1024]{2,1,0:T(8,128)S(1)} %get-tuple-element.295, s32[512]{0:T(512)S(1)} %bitcast.127), kind=kOutput, calls=%fused_computation.4.clone.1 | convolution fusion | flops 1211136512 | bytes 1318912 | tf_op jit(solution)/shard_map/while/body/eval_jaxpr/sr,frc->fsc/dot_general | solution.py:87
  131.5 3.7 %select_reduce_fusion.2 = f32[512,3]{0,1:T(4,128)S(1)} fusion(pred[512,1024]{1,0:T(8,128)(4,1)S(1)} %iota_compare_fusion.6, f32[3,64,1024]{2,1,0:T(8,128)S(1)} %get-tuple-element.295, s32[512]{0:T(512)S(1)} %bitcast.127), kind=kOutput, calls=%fused_computation.4.clone.1 | convolution fusion | flops 1211136512 | bytes 1318912 | tf_op jit(solution)/shard_map/while/body/eval_jaxpr/sr,frc->fsc/dot_general | solution.py:87
  136.3 3.6 %select_reduce_fusion.2 = f32[512,3]{0,1:T(4,128)S(1)} fusion(pred[512,1024]{1,0:T(8,128)(4,1)S(1)} %iota_compare_fusion.6, f32[3,64,1024]{2,1,0:T(8,128)S(1)} %get-tuple-element.295, s32[512]{0:T(512)S(1)} %bitcast.127), kind=kOutput, calls=%fused_computation.4.clone.1 | convolution fusion | flops 1211136512 | bytes 1318912 | tf_op jit(solution)/shard_map/while/body/eval_jaxpr/sr,frc->fsc/dot_general | solution.py:87
  141.1 3.7 %select_reduce_fusion.2 = f32[512,3]{0,1:T(4,128)S(1)} fusion(pred[512,1024]{1,0:T(8,128)(4,1)S(1)} %iota_compare_fusion.6, f32[3,64,1024]{2,1,0:T(8,128)S(1)} %get-tuple-element.295, s32[512]{0:T(512)S(1)} %bitcast.127), kind=kOutput, calls=%fused_computation.4.clone.1 | convolution fusion | flops 1211136512 | bytes 1318912 | tf_op jit(solution)/shard_map/while/body/eval_jaxpr/sr,frc->fsc/dot_general | solution.py:87
  145.9 3.6 %select_reduce_fusion.2 = f32[512,3]{0,1:T(4,128)S(1)} fusion(pred[512,1024]{1,0:T(8,128)(4,1)S(1)} %iota_compare_fusion.6, f32[3,64,1024]{2,1,0:T(8,128)S(1)} %get-tuple-element.295, s32[512]{0:T(512)S(1)} %bitcast.127), kind=kOutput, calls=%fused_computation.4.clone.1 | convolution fusion | flops 1211136512 | bytes 1318912 | tf_op jit(solution)/shard_map/while/body/eval_jaxpr/sr,frc->fsc/dot_general | solution.py:87
  150.7 3.7 %select_reduce_fusion.2 = f32[512,3]{0,1:T(4,128)S(1)} fusion(pred[512,1024]{1,0:T(8,128)(4,1)S(1)} %iota_compare_fusion.6, f32[3,64,1024]{2,1,0:T(8,128)S(1)} %get-tuple-element.295, s32[512]{0:T(512)S(1)} %bitcast.127), kind=kOutput, calls=%fused_computation.4.clone.1 | convolution fusion | flops 1211136512 | bytes 1318912 | tf_op jit(solution)/shard_map/while/body/eval_jaxpr/sr,frc->fsc/dot_general | solution.py:87
  155.5 3.6 %select_reduce_fusion.2 = f32[512,3]{0,1:T(4,128)S(1)} fusion(pred[512,1024]{1,0:T(8,128)(4,1)S(1)} %iota_compare_fusion.6, f32[3,64,1024]{2,1,0:T(8,128)S(1)} %get-tuple-element.295, s32[512]{0:T(512)S(1)} %bitcast.127), kind=kOutput, calls=%fused_computation.4.clone.1 | convolution fusion | flops 1211136512 | bytes 1318912 | tf_op jit(solution)/shard_map/while/body/eval_jaxpr/sr,frc->fsc/dot_general | solution.py:87
  160.3 3.7 %select_reduce_fusion.2 = f32[512,3]{0,1:T(4,128)S(1)} fusion(pred[512,1024]{1,0:T(8,128)(4,1)S(1)} %iota_compare_fusion.6, f32[3,64,1024]{2,1,0:T(8,128)S(1)} %get-tuple-element.295, s32[512]{0:T(512)S(1)} %bitcast.127), kind=kOutput, calls=%fused_computation.4.clone.1 | convolution fusion | flops 1211136512 | bytes 1318912 | tf_op jit(solution)/shard_map/while/body/eval_jaxpr/sr,frc->fsc/dot_general | solution.py:87
  165.1 3.6 %select_reduce_fusion.2 = f32[512,3]{0,1:T(4,128)S(1)} fusion(pred[512,1024]{1,0:T(8,128)(4,1)S(1)} %iota_compare_fusion.6, f32[3,64,1024]{2,1,0:T(8,128)S(1)} %get-tuple-element.295, s32[512]{0:T(512)S(1)} %bitcast.127), kind=kOutput, calls=%fused_computation.4.clone.1 | convolution fusion | flops 1211136512 | bytes 1318912 | tf_op jit(solution)/shard_map/while/body/eval_jaxpr/sr,frc->fsc/dot_general | solution.py:87
  169.9 3.7 %select_reduce_fusion.2 = f32[512,3]{0,1:T(4,128)S(1)} fusion(pred[512,1024]{1,0:T(8,128)(4,1)S(1)} %iota_compare_fusion.6, f32[3,64,1024]{2,1,0:T(8,128)S(1)} %get-tuple-element.295, s32[512]{0:T(512)S(1)} %bitcast.127), kind=kOutput, calls=%fused_computation.4.clone.1 | convolution fusion | flops 1211136512 | bytes 1318912 | tf_op jit(solution)/shard_map/while/body/eval_jaxpr/sr,frc->fsc/dot_general | solution.py:87
  173.9 27.4 %while.23 = (s32[]{:T(128)}, f32[2,16,1024]{2,1,0:T(8,128)S(1)}, s32[16,512]{1,0:T(8,128)}, f32[16,2,512]{2,1,0:T(2,128)S(1)}, s32[16,512]{1,0:T(8,128)}, /*index=5*/s32[]{:T(128)}, s32[]{:T(128)}) while((s32[]{:T(128)}, f32[2,16,1024]{2,1,0:T(8,128)S(1)}, s32[16,512]{1,0:T(8,128)}, f32[16,2,512]{2,1,0:T(2,128)S(1)}, ...), condition=%wide.region_4.5_spmd.clone, body=%wide.region_3.4_spmd.clone.sunk | while | flops 201949184 | bytes 352359 | solution.py:157
  201.3 4.7 %copy.15 = f32[2,16,1024]{0,2,1:T(8,128)} copy(f32[2,16,1024]{2,1,0:T(8,128)S(1)} %get-tuple-element.78) | data formatting | bytes 262144
  206.9 103.0 %reduce-scatter.4.cloned.1.call-done = f32[1024,2]{1,0:T(8,128)} async-done(((f32[16384,2]{1,0:T(8,128)}), f32[1024,2]{1,0:T(8,128)}) %reduce-scatter.4.cloned.1.call-update) | async-done | bytes 8208
  (247 shorter events, 95.2 us)
Async XLA Ops:
  7.2 302.8 %reduce-scatter.4.cloned.1.call-start = ((), (), s32[]{:S(2)}) async-start(), calls=%async_computation.1 | async-start | bytes 8912896
  8.0 10.9 %collective-permute-start.4 = (f32[1,1,1024]{2,1,0:T(1,128)S(1)}, f32[1,1,1024]{2,1,0:T(1,128)S(1)}, u32[]{:S(2)}, u32[]{:S(2)}) collective-permute-start(f32[1,1,1024]{2,1,0:T(1,128)S(1)} %get-tuple-element.194), channel_id=1, source_target_pairs={{0,1},{1,2},{2,3},{4,5},{5,6},{6,7},{8,9},{9,10},{10,11},{12,13},{... | collective-permute-start | bytes 12296 | tf_op jit(solution)/shard_map/ppermute | solution.py:23
  10.3 8.6 %collective-permute-start.5 = (f32[1,1,1024]{2,1,0:T(1,128)S(1)}, f32[1,1,1024]{2,1,0:T(1,128)S(1)}, u32[]{:S(2)}, u32[]{:S(2)}) collective-permute-start(f32[1,1,1024]{2,1,0:T(1,128)S(1)} %get-tuple-element.195), channel_id=1, source_target_pairs={{1,0},{2,1},{3,2},{5,4},{6,5},{7,6},{9,8},{10,9},{11,10},{13,12},{... | collective-permute-start | bytes 12296 | tf_op jit(solution)/shard_map/ppermute | solution.py:24
  12.4 17.5 %collective-permute-start = (f32[3,1,1024]{2,1,0:T(1,128)S(1)}, f32[3,1,1024]{2,1,0:T(1,128)S(1)}, u32[]{:S(2)}, u32[]{:S(2)}) collective-permute-start(f32[3,1,1024]{2,1,0:T(1,128)S(1)} %get-tuple-element.196), channel_id=1, source_target_pairs={{0,1},{1,2},{2,3},{4,5},{5,6},{6,7},{8,9},{9,10},{10,11},{12,13},{... | collective-permute-start | bytes 36872 | tf_op jit(solution)/shard_map/ppermute | solution.py:23
  17.6 12.4 %collective-permute-start.1 = (f32[3,1,1024]{2,1,0:T(1,128)S(1)}, f32[3,1,1024]{2,1,0:T(1,128)S(1)}, u32[]{:S(2)}, u32[]{:S(2)}) collective-permute-start(f32[3,1,1024]{2,1,0:T(1,128)S(1)} %get-tuple-element.197), channel_id=1, source_target_pairs={{1,0},{2,1},{3,2},{5,4},{6,5},{7,6},{9,8},{10,9},{11,10},{13,12},{... | collective-permute-start | bytes 36872 | tf_op jit(solution)/shard_map/ppermute | solution.py:24
  20.0 5.2 %collective-permute-start.7 = (f32[1,66,1]{2,1,0:T(8,128)S(1)}, f32[1,66,1]{2,1,0:T(8,128)S(1)}, u32[]{:S(2)}, u32[]{:S(2)}) collective-permute-start(f32[1,66,1]{2,1,0:T(8,128)S(1)} %get-tuple-element.192), channel_id=1, source_target_pairs={{4,0},{8,4},{12,8},{0,12},{5,1},{9,5},{13,9},{1,13},{6,2},{10,6},{... | collective-permute-start | bytes 800 | tf_op jit(solution)/shard_map/ppermute | solution.py:24
  23.6 5.8 %collective-permute-start.6 = (f32[1,66,1]{2,1,0:T(8,128)S(1)}, f32[1,66,1]{2,1,0:T(8,128)S(1)}, u32[]{:S(2)}, u32[]{:S(2)}) collective-permute-start(f32[1,66,1]{2,1,0:T(8,128)S(1)} %get-tuple-element.193), channel_id=1, source_target_pairs={{0,4},{4,8},{8,12},{12,0},{1,5},{5,9},{9,13},{13,1},{2,6},{6,10},{... | collective-permute-start | bytes 800 | tf_op jit(solution)/shard_map/ppermute | solution.py:23
  30.2 8.3 %collective-permute-start.3 = (f32[3,66,1]{2,1,0:T(8,128)S(1)}, f32[3,66,1]{2,1,0:T(8,128)S(1)}, u32[]{:S(2)}, u32[]{:S(2)}) collective-permute-start(f32[3,66,1]{2,1,0:T(8,128)S(1)} %get-tuple-element.180), channel_id=1, source_target_pairs={{4,0},{8,4},{12,8},{0,12},{5,1},{9,5},{13,9},{1,13},{6,2},{10,6},{... | collective-permute-start | bytes 2384 | tf_op jit(solution)/shard_map/ppermute | solution.py:24
  30.3 8.2 %collective-permute-start.2 = (f32[3,66,1]{2,1,0:T(8,128)S(1)}, f32[3,66,1]{2,1,0:T(8,128)S(1)}, u32[]{:S(2)}, u32[]{:S(2)}) collective-permute-start(f32[3,66,1]{2,1,0:T(8,128)S(1)} %get-tuple-element.181), channel_id=1, source_target_pairs={{0,4},{4,8},{8,12},{12,0},{1,5},{5,9},{9,13},{13,1},{2,6},{6,10},{... | collective-permute-start | bytes 2384 | tf_op jit(solution)/shard_map/ppermute | solution.py:23
  41.8 7.8 %copy-start.1 = (f32[65,1024]{1,0:T(8,128)}, f32[65,1024]{1,0:T(8,128)S(1)}, u32[]{:S(2)}) copy-start(f32[65,1024]{1,0:T(8,128)S(1)} %get-tuple-element.152) | copy-start | bytes 798724
  42.2 3.3 %collective-permute-start.8 = (f32[3,1,1024]{2,1,0:T(1,128)S(1)}, f32[3,1,1024]{2,1,0:T(1,128)S(1)}, u32[]{:S(2)}, u32[]{:S(2)}) collective-permute-start(f32[3,1,1024]{2,1,0:T(1,128)S(1)} %get-tuple-element.186), channel_id=1, source_target_pairs={{0,1},{1,2},{2,3},{4,5},{5,6},{6,7},{8,9},{9,10},{10,11},{12,13},{... | collective-permute-start | bytes 36872 | tf_op jit(solution)/shard_map/ppermute | solution.py:23
  44.2 5.3 %collective-permute-start.9 = (f32[3,1,1024]{2,1,0:T(1,128)S(1)}, f32[3,1,1024]{2,1,0:T(1,128)S(1)}, u32[]{:S(2)}, u32[]{:S(2)}) collective-permute-start(f32[3,1,1024]{2,1,0:T(1,128)S(1)} %get-tuple-element.187), channel_id=1, source_target_pairs={{1,0},{2,1},{3,2},{5,4},{6,5},{7,6},{9,8},{10,9},{11,10},{13,12},{... | collective-permute-start | bytes 36872 | tf_op jit(solution)/shard_map/ppermute | solution.py:24
  49.7 4.8 %collective-permute-start.11 = (f32[3,66,1]{2,1,0:T(8,128)S(1)}, f32[3,66,1]{2,1,0:T(8,128)S(1)}, u32[]{:S(2)}, u32[]{:S(2)}) collective-permute-start(f32[3,66,1]{2,1,0:T(8,128)S(1)} %get-tuple-element.178), channel_id=1, source_target_pairs={{4,0},{8,4},{12,8},{0,12},{5,1},{9,5},{13,9},{1,13},{6,2},{10,6},{... | collective-permute-start | bytes 2384 | tf_op jit(solution)/shard_map/ppermute | solution.py:24
  49.8 7.3 %collective-permute-start.10 = (f32[3,66,1]{2,1,0:T(8,128)S(1)}, f32[3,66,1]{2,1,0:T(8,128)}, u32[]{:S(2)}, u32[]{:S(2)}) collective-permute-start(f32[3,66,1]{2,1,0:T(8,128)S(1)} %get-tuple-element.179), channel_id=1, source_target_pairs={{0,4},{4,8},{8,12},{12,0},{1,5},{5,9},{9,13},{13,1},{2,6},{6,10},{... | collective-permute-start | bytes 2384 | tf_op jit(solution)/shard_map/ppermute | solution.py:23
  59.6 4.3 %collective-permute-start.12 = (f32[3,1,1024]{2,1,0:T(1,128)S(1)}, f32[3,1,1024]{2,1,0:T(1,128)S(1)}, u32[]{:S(2)}, u32[]{:S(2)}) collective-permute-start(f32[3,1,1024]{2,1,0:T(1,128)S(1)} %get-tuple-element.184), channel_id=1, source_target_pairs={{0,1},{1,2},{2,3},{4,5},{5,6},{6,7},{8,9},{9,10},{10,11},{12,13},{... | collective-permute-start | bytes 36872 | tf_op jit(solution)/shard_map/ppermute | solution.py:23
  62.6 3.4 %collective-permute-start.13 = (f32[3,1,1024]{2,1,0:T(1,128)S(1)}, f32[3,1,1024]{2,1,0:T(1,128)S(1)}, u32[]{:S(2)}, u32[]{:S(2)}) collective-permute-start(f32[3,1,1024]{2,1,0:T(1,128)S(1)} %get-tuple-element.185), channel_id=1, source_target_pairs={{1,0},{2,1},{3,2},{5,4},{6,5},{7,6},{9,8},{10,9},{11,10},{13,12},{... | collective-permute-start | bytes 36872 | tf_op jit(solution)/shard_map/ppermute | solution.py:24
  66.2 4.8 %collective-permute-start.15 = (f32[3,66,1]{2,1,0:T(8,128)S(1)}, f32[3,66,1]{2,1,0:T(8,128)S(1)}, u32[]{:S(2)}, u32[]{:S(2)}) collective-permute-start(f32[3,66,1]{2,1,0:T(8,128)S(1)} %get-tuple-element.176), channel_id=1, source_target_pairs={{4,0},{8,4},{12,8},{0,12},{5,1},{9,5},{13,9},{1,13},{6,2},{10,6},{... | collective-permute-start | bytes 2384 | tf_op jit(solution)/shard_map/ppermute | solution.py:24
  67.5 6.8 %collective-permute-start.14 = (f32[3,66,1]{2,1,0:T(8,128)S(1)}, f32[3,66,1]{2,1,0:T(8,128)S(1)}, u32[]{:S(2)}, u32[]{:S(2)}) collective-permute-start(f32[3,66,1]{2,1,0:T(8,128)S(1)} %get-tuple-element.177), channel_id=1, source_target_pairs={{0,4},{4,8},{8,12},{12,0},{1,5},{5,9},{9,13},{13,1},{2,6},{6,10},{... | collective-permute-start | bytes 2384 | tf_op jit(solution)/shard_map/ppermute | solution.py:23
  77.9 5.2 %copy-start.11 = (s32[8192]{0:T(1024)S(1)}, s32[8192]{0:T(1024)}, u32[]{:S(2)}) copy-start(s32[8192]{0:T(1024)} %param.16) | copy-start | bytes 98308
  79.2 9.4 %copy-start.14 = (s32[8192]{0:T(1024)S(1)}, s32[8192]{0:T(1024)}, u32[]{:S(2)}) copy-start(s32[8192]{0:T(1024)} %param.17) | copy-start | bytes 98308
  79.2 10.0 %copy-start.15 = (s32[8192]{0:T(1024)S(1)}, s32[8192]{0:T(1024)}, u32[]{:S(2)}) copy-start(s32[8192]{0:T(1024)} %param.18) | copy-start | bytes 98308
  79.2 4.0 %collective-permute-start.16 = (f32[3,1,1024]{2,1,0:T(1,128)S(1)}, f32[3,1,1024]{2,1,0:T(1,128)S(1)}, u32[]{:S(2)}, u32[]{:S(2)}) collective-permute-start(f32[3,1,1024]{2,1,0:T(1,128)S(1)} %get-tuple-element.182), channel_id=1, source_target_pairs={{0,1},{1,2},{2,3},{4,5},{5,6},{6,7},{8,9},{9,10},{10,11},{12,13},{... | collective-permute-start | bytes 36872 | tf_op jit(solution)/shard_map/ppermute | solution.py:23
  81.9 3.8 %collective-permute-start.17 = (f32[3,1,1024]{2,1,0:T(1,128)S(1)}, f32[3,1,1024]{2,1,0:T(1,128)S(1)}, u32[]{:S(2)}, u32[]{:S(2)}) collective-permute-start(f32[3,1,1024]{2,1,0:T(1,128)S(1)} %get-tuple-element.183), channel_id=1, source_target_pairs={{1,0},{2,1},{3,2},{5,4},{6,5},{7,6},{9,8},{10,9},{11,10},{13,12},{... | collective-permute-start | bytes 36872 | tf_op jit(solution)/shard_map/ppermute | solution.py:24
  85.8 5.2 %collective-permute-start.19 = (f32[3,66,1]{2,1,0:T(8,128)S(1)}, f32[3,66,1]{2,1,0:T(8,128)S(1)}, u32[]{:S(2)}, u32[]{:S(2)}) collective-permute-start(f32[3,66,1]{2,1,0:T(8,128)S(1)} %get-tuple-element.174), channel_id=1, source_target_pairs={{4,0},{8,4},{12,8},{0,12},{5,1},{9,5},{13,9},{1,13},{6,2},{10,6},{... | collective-permute-start | bytes 2384 | tf_op jit(solution)/shard_map/ppermute | solution.py:24
  86.4 6.8 %collective-permute-start.18 = (f32[3,66,1]{2,1,0:T(8,128)S(1)}, f32[3,66,1]{2,1,0:T(8,128)}, u32[]{:S(2)}, u32[]{:S(2)}) collective-permute-start(f32[3,66,1]{2,1,0:T(8,128)S(1)} %get-tuple-element.175), channel_id=1, source_target_pairs={{0,4},{4,8},{8,12},{12,0},{1,5},{5,9},{9,13},{13,1},{2,6},{6,10},{... | collective-permute-start | bytes 2384 | tf_op jit(solution)/shard_map/ppermute | solution.py:23
  94.6 1.6 copy-start.2
  94.7 1.6 copy-start.6
  96.8 76.8 %copy-start.12 = (f32[8192]{0:T(1024)S(1)}, f32[8192]{0:T(1024)}, u32[]{:S(2)}) copy-start(f32[8192]{0:T(1024)} %param.19) | copy-start | bytes 98308
  96.8 76.9 %copy-start.13 = (f32[8192]{0:T(1024)S(1)}, f32[8192]{0:T(1024)}, u32[]{:S(2)}) copy-start(f32[8192]{0:T(1024)} %param.20) | copy-start | bytes 98308
  96.8 77.1 %copy-start.9 = (f32[2,16,1024]{2,1,0:T(8,128)S(1)}, f32[2,16,1024]{2,1,0:T(8,128)}, u32[]{:S(2)}) copy-start(f32[2,16,1024]{2,1,0:T(8,128)} %custom-call) | copy-start | bytes 393220
  206.0 105.7 %copy-start.16 = (f32[1024]{0:T(1024)S(1)}, f32[1024]{0:T(1024)}, u32[]{:S(2)}) copy-start(f32[1024]{0:T(1024)} %param.23) | copy-start | bytes 12292
  206.0 105.7 %copy-start.17 = (f32[1024]{0:T(1024)S(1)}, f32[1024]{0:T(1024)}, u32[]{:S(2)}) copy-start(f32[1024]{0:T(1024)} %param.22) | copy-start | bytes 12292
  (7 other events, 7.1 us)
Sparse Core Ops, SparseCore 0:
  206.1 103.7 reduce-scatter.3
where the time goes:
time: 326 us; the launch traced here: 319 us
  waiting for transfers between devices  135 us (41%)
  matrix products  73.1 us (22%)
  local copies, waits for them, and re-layouts  46.2 us (14%)
  starting transfers between devices  33.5 us (10%)
  between operations  15.3 us (5%)
  other arithmetic  15.1 us (5%)
    unnamed x2, waiting for transfers between devices  103 us
    dot_general x16, matrix products, one_block(): picked = jnp.einsum('sr,frc->fsc', row_hot, fields, precision=EXACT)  58.4 us
    dynamic_slice x32, local copies, waits for them, and re-layouts, sample_values(): values = lax.map(one_block, (cell_rows, cell_cols))  24 us
    ppermute x10, starting transfers between devices, padded(): before = lax.ppermute(last, axis, up)  21.2 us
    ppermute x10, waiting for transfers between devices, padded(): after = lax.ppermute(leading, axis, down)  19.8 us
    dot_general x16, matrix products, add_block(): jnp.einsum('tso,sr->tor', weighted, reach_hot, precision=EXACT)  14.7 us
    ppermute x10, starting transfers between devices, padded(): after = lax.ppermute(leading, axis, down)  12.2 us
    ppermute x10, waiting for transfers between devices, padded(): before = lax.ppermute(last, axis, up)  12.2 us
  transfers between devices with their start and end apart: 21, of which 12 were waited for; matrix products, arithmetic and copies ran while one was open for 2% of the time, Pallas kernels for 0%

commit v1 on v0

v1 whole, which is shorter than its diff:
```python
import functools

import jax
import jax.numpy as jnp
from jax import lax
from jax.experimental import pallas as pl
from jax.experimental.pallas import tpu as pltpu
from jax.sharding import PartitionSpec as P

STEPS = 4
WAVE_GAIN = 0.2
DRAG_RATE = 0.05
MESH = pl.DeviceIdType.MESH
PAD_R = 8
PAD_C = 128
LANES = 128
GROUP = 8
TABLE = 256


def split(value):
    high = value.astype(jnp.bfloat16).astype(jnp.float32)
    return high, value - high


def kernel(
    dims,
    bed_ref,
    cot_ref,
    cell_ref,
    owner_ref,
    reach_ref,
    weight_ref,
    angle_ref,
    count_ref,
    width_ref,
    rbed_ref,
    level_out,
    gwidth_out,
    gbed_out,
    bed,
    lev,
    fields,
    hot,
    terms,
    spots,
    sums,
    recv,
    weights,
    halo_send,
    halo_recv,
    send_sem,
    recv_sem,
):
    n_lon, n_lat, rows, cols = dims
    owners = n_lon * n_lat
    lon, lat = lax.axis_index("lon"), lax.axis_index("lat")
    me = lon * n_lat + lat
    tall, wide = rows + 2 * PAD_R, cols + 2 * PAD_C
    slot_rows = cell_ref.shape[0]

    barrier = pltpu.get_barrier_semaphore()

    def peer(step):
        other = lax.rem(me + step, owners)
        return {"lon": other // n_lat, "lat": lax.rem(other, n_lat)}

    def greet(step, carry):
        pl.semaphore_signal(barrier, inc=1, device_id=peer(step), device_id_type=MESH)
        return carry

    lax.fori_loop(1, owners, greet, 0)
    lev[PAD_R : PAD_R + rows, PAD_C : PAD_C + cols] = cot_ref[...]
    bed[PAD_R : PAD_R + rows, PAD_C : PAD_C + cols] = bed_ref[...]
    pl.semaphore_wait(barrier, owners - 1)

    def span(step, length, pad):
        if step == 0:
            return pl.ds(0, length), pl.ds(pad, length)
        if step > 0:
            return pl.ds(length - pad, pad), pl.ds(0, pad)
        return pl.ds(0, pad), pl.ds(pad + length, pad)

    copies = []
    for d_lon, d_lat in ((1, 0), (-1, 0), (1, 1), (1, -1), (-1, 1), (-1, -1), (0, 1), (0, -1)):
        from_r, to_r = span(d_lat, rows, PAD_R)
        from_c, to_c = span(d_lon, cols, PAD_C)
        target = {
            "lon": lax.rem(lon + d_lon + n_lon, n_lon),
            "lat": lax.rem(lat + d_lat + n_lat, n_lat),
        }
        for source, place in ((bed_ref, bed), (cot_ref, lev)):
            index = len(copies)
            copy = pltpu.make_async_remote_copy(
                src_ref=source.at[from_r, from_c],
                dst_ref=place.at[to_r, to_c],
                send_sem=halo_send.at[index],
                recv_sem=halo_recv.at[index],
                device_id=target,
                device_id_type=MESH,
            )
            copy.start()
            copies.append(copy)

    slot = (
        lax.broadcasted_iota(jnp.int32, (slot_rows, LANES), 0) * LANES
        + lax.broadcasted_iota(jnp.int32, (slot_rows, LANES), 1)
    )
    weight = jnp.where(slot < count_ref[0], weight_ref[...], 0.0)
    angle = angle_ref[...]
    weights[0] = weight
    weights[1] = weight * jnp.cos(angle)
    weights[2] = weight * jnp.sin(angle)
    sums[...] = jnp.zeros_like(sums)

    for copy in copies:
        copy.wait()

    def east(value):
        return pltpu.roll(value, wide - 1, 1)

    def west(value):
        return pltpu.roll(value, 1, 1)

    def north(value):
        return pltpu.roll(value, tall - 1, 0)

    def south(value):
        return pltpu.roll(value, 1, 0)

    row = lat * rows - PAD_R + lax.broadcasted_iota(jnp.int32, (tall, wide), 0)
    open_north = (row >= 0) & (row < n_lat * rows - 1)
    depth = bed[...]
    east_depth = 0.5 * (depth + east(depth))
    north_depth = 0.5 * (depth + north(depth))
    east_keep = east_depth / (east_depth + DRAG_RATE)
    north_keep = jnp.where(open_north, north_depth / (north_depth + DRAG_RATE), 0.0)
    east_gain = WAVE_GAIN * east_keep * east_depth
    north_gain = WAVE_GAIN * north_keep * north_depth
    level = lev[...]
    sum_level = level
    for step in range(STEPS):
        east_mid = east(level) - level
        north_mid = north(level) - level
        if step > 0:
            sum_level = sum_level + level
            east_mid = east_mid + east_adj
            north_mid = north_mid + north_adj
        north_mid = jnp.where(open_north, north_mid, 0.0)
        east_flux = east_gain * east_mid
        north_flux = north_gain * north_mid
        level = level + east_flux - west(east_flux) + north_flux - south(north_flux)
        if step == 0:
            sum_east, sum_north = east_mid, north_mid
        else:
            sum_east, sum_north = sum_east + east_mid, sum_north + north_mid
        if step + 1 < STEPS:
            east_adj = east_keep * east_mid
            north_adj = north_keep * north_mid
    level_out[...] = level[PAD_R : PAD_R + rows, PAD_C : PAD_C + cols]

    half = cols // 2
    picks = 2 * rows
    for index, value in enumerate((sum_level, sum_east, sum_north)):
        for side in range(2):
            first = PAD_C + side * half
            high, low = split(value[PAD_R : PAD_R + rows, first : first + half])
            place = slice(index * picks + side * rows, index * picks + (side + 1) * rows)
            fields[place, 0:half] = high.astype(jnp.bfloat16)
            fields[place, half : 2 * half] = low.astype(jnp.bfloat16)

    reach_rows = width_ref.shape[0] // 2
    per_owner = 2 * reach_rows
    table = owners * per_owner
    block = GROUP * LANES

    def one_block(number, carry):
        here = pl.ds(pl.multiple_of(number * GROUP, GROUP), GROUP)
        cell = cell_ref[here, :]
        column = cell % cols
        deep = column % half
        pick = (column // half) * rows + cell // cols
        reach = reach_ref[here, :]
        tile = reach // LANES
        key = owner_ref[here, :] * reach_rows + tile % reach_rows
        lane = (tile // reach_rows) * LANES + reach % LANES
        for_level, for_east, for_north = (weights[i, here, :] for i in range(3))
        deep_ids = lax.broadcasted_iota(jnp.int32, (half, LANES), 0)
        pick_ids = lax.broadcasted_iota(jnp.int32, (picks, LANES), 0)
        lane_ids = lax.broadcasted_iota(jnp.int32, (TABLE, LANES), 0)
        line_ids = lax.broadcasted_iota(jnp.int32, (table, LANES), 0)
        key_ids = (line_ids // per_owner) * reach_rows + line_ids % reach_rows
        is_flow = (line_ids // reach_rows) % 2 == 1
        for i in range(GROUP):
            at = slice(i * LANES, (i + 1) * LANES)
            hot[:, at] = jnp.where(deep_ids == deep[i : i + 1], 1.0, 0.0).astype(jnp.bfloat16)
            spots[:, at] = jnp.where(lane_ids == lane[i : i + 1], 1.0, 0.0).astype(jnp.bfloat16)
        found = jnp.dot(
            fields[:, 0:half], hot[...], preferred_element_type=jnp.float32
        ) + jnp.dot(fields[:, half : 2 * half], hot[...], preferred_element_type=jnp.float32)
        for i in range(GROUP):
            at = slice(i * LANES, (i + 1) * LANES)
            mine = pick_ids == pick[i : i + 1]
            value = [
                jnp.sum(
                    jnp.where(mine, found[f * picks : (f + 1) * picks, at], 0.0),
                    axis=0,
                    keepdims=True,
                )
                for f in range(3)
            ]
            level_high, level_low = split(for_level[i : i + 1] * value[0])
            flow_high, flow_low = split(
                for_east[i : i + 1] * value[1] + for_north[i : i + 1] * value[2]
            )
            line = key_ids == key[i : i + 1]
            terms[0:table, at] = jnp.where(
                line, jnp.where(is_flow, flow_high, level_high), 0.0
            ).astype(jnp.bfloat16)
            terms[table : 2 * table, at] = jnp.where(
                line, jnp.where(is_flow, flow_low, level_low), 0.0
            ).astype(jnp.bfloat16)
        added = lax.dot_general(
            terms[...], spots[...], (((1,), (1,)), ((), ())), preferred_element_type=jnp.float32
        )
        sums[...] += added[0:table] + added[table : 2 * table]
        return carry

    lax.fori_loop(0, slot_rows * LANES // block, one_block, 0)

    def outgoing(step):
        other = lax.rem(me + step, owners)
        return pltpu.make_async_remote_copy(
            src_ref=sums.at[pl.ds(pl.multiple_of(other * per_owner, per_owner), per_owner)],
            dst_ref=recv.at[step],
            send_sem=send_sem.at[step],
            recv_sem=recv_sem.at[step],
            device_id=peer(step),
            device_id_type=MESH,
        )

    def send(step, carry):
        outgoing(step).start()
        return carry

    def take(step, total):
        outgoing(step).wait()
        return total + recv[step]

    lax.fori_loop(1, owners, send, 0)
    own = sums[pl.ds(pl.multiple_of(me * per_owner, per_owner), per_owner), :]
    total = lax.fori_loop(1, owners, take, own)
    level_total = jnp.concatenate(
        [total[0:reach_rows, 0:LANES], total[0:reach_rows, LANES:TABLE]], axis=0
    )
    flow_total = jnp.concatenate(
        [total[reach_rows:per_owner, 0:LANES], total[reach_rows:per_owner, LANES:TABLE]], axis=0
    )
    gwidth_out[...] = rbed_ref[...] * level_total
    gbed_out[...] = width_ref[...] * level_total + rbed_ref[...] * flow_total


def on_device(
    dims,
    bed_depth,
    cotangent,
    sample_cell,
    sample_owner,
    sample_reach,
    sample_weight,
    sample_angle,
    sample_count,
    reach_width,
    reach_bed,
):
    n_lon, n_lat = dims
    rows, cols = bed_depth.shape
    owners = n_lon * n_lat
    tall, wide = rows + 2 * PAD_R, cols + 2 * PAD_C
    slot_rows = sample_cell.shape[0] // LANES
    reach_tiles = reach_width.shape[0] // LANES
    per_owner = reach_tiles
    block = GROUP * LANES

    def tiled(value):
        return value.reshape(-1, LANES)

    vmem = pl.BlockSpec(memory_space=pltpu.VMEM)
    level, gwidth, gbed = pl.pallas_call(
        functools.partial(kernel, (n_lon, n_lat, rows, cols)),
        out_shape=(
            jax.ShapeDtypeStruct((rows, cols), jnp.float32),
            jax.ShapeDtypeStruct((reach_tiles, LANES), jnp.float32),
            jax.ShapeDtypeStruct((reach_tiles, LANES), jnp.float32),
        ),
        in_specs=[vmem] * 7 + [pl.BlockSpec(memory_space=pltpu.SMEM)] + [vmem] * 2,
        out_specs=(vmem, vmem, vmem),
        scratch_shapes=[
            pltpu.VMEM((tall, wide), jnp.float32),
            pltpu.VMEM((tall, wide), jnp.float32),
            pltpu.VMEM((6 * rows, cols), jnp.bfloat16),
            pltpu.VMEM((cols // 2, block), jnp.bfloat16),
            pltpu.VMEM((2 * owners * per_owner, block), jnp.bfloat16),
            pltpu.VMEM((TABLE, block), jnp.bfloat16),
            pltpu.VMEM((owners * per_owner, TABLE), jnp.float32),
            pltpu.VMEM((owners, per_owner, TABLE), jnp.float32),
            pltpu.VMEM((3, slot_rows, LANES), jnp.float32),
            pltpu.SemaphoreType.DMA((16,)),
            pltpu.SemaphoreType.DMA((16,)),
            pltpu.SemaphoreType.DMA((owners,)),
            pltpu.SemaphoreType.DMA((owners,)),
        ],
        compiler_params=pltpu.CompilerParams(
            collective_id=0, has_side_effects=True, vmem_limit_bytes=48 << 20
        ),
    )(
        bed_depth,
        cotangent,
        tiled(sample_cell),
        tiled(sample_owner),
        tiled(sample_reach),
        tiled(sample_weight),
        tiled(sample_angle),
        sample_count,
        tiled(reach_width),
        tiled(reach_bed),
    )
    return level, gwidth.reshape(-1), gbed.reshape(-1)


def solution(mesh):
    flat = P(("lon", "lat"))
    return jax.shard_map(
        functools.partial(on_device, (mesh.shape["lon"], mesh.shape["lat"])),
        mesh=mesh,
        in_specs=(P("lat", "lon"), P(("ens", "lat"), "lon")) + (flat,) * 8,
        out_specs=(P(("ens", "lat"), "lon"), P(("ens", "lon", "lat")), P(("ens", "lon", "lat"))),
        check_vma=False,
    )
```

time: 326 us -> 41.8 us (0.13); the launches traced: 319 us -> 41.2 us
  waiting for transfers between devices: 135 us -> 0 us
  matrix products: 73.1 us -> 0 us
  local copies, waits for them, and re-layouts: 46.2 us -> 8.26 us
  starting transfers between devices: 33.5 us -> 0 us
  Pallas kernels: 0 us -> 31.7 us
  other arithmetic: 15.1 us -> 0 us
  between operations: 15.3 us -> 1.31 us
    unnamed x2 -> x0, waiting for transfers between devices: 103 us -> none
    dot_general x32 -> x0, matrix products: 73.1 us -> none  [the longest x16 58.4 us: one_block(): picked = jnp.einsum('sr,frc->fsc', row_hot, fields, precision=EXACT)]
    ppermute x20 -> x0, starting transfers between devices: 33.5 us -> none  [the longest x10 21.2 us: padded(): before = lax.ppermute(last, axis, up)]
    ppermute x20 -> x0, waiting for transfers between devices: 32 us -> none  [the longest x10 19.8 us: padded(): after = lax.ppermute(leading, axis, down)]
    pallas_call x0 -> x1, Pallas kernels: none -> 31.7 us  [on_device(): pl.pallas_call(functools.partial(kernel, (n_lon, n_lat, rows, cols)), out...]
    dynamic_slice x32 -> x0, local copies, waits for them, and re-layouts: 24 us -> none  [sample_values(): values = lax.map(one_block, (cell_rows, cell_cols))]
    eq x16 -> x0, other arithmetic: 5.75 us -> none  [one_block(): col_hot = (cols_here[:, None] == col_ids[None, :])[None]]
    concatenate x5 -> x0, local copies, waits for them, and re-layouts: 5.35 us -> none  [padded(): value = jnp.concatenate([before, value, after], axis=dim)]
  transfers between devices with their start and end apart: 21 -> 0, of which waited for: 12 -> 0; matrix products, arithmetic and copies ran while one was open for 2% -> 0% of each run, Pallas kernels for 0% -> 0%
where the time goes in v1:
time: 41.8 us; the launch traced here: 41.2 us
  Pallas kernels  31.7 us (76%)
  local copies, waits for them, and re-layouts  8.26 us (20%)
  between operations  1.31 us (3%)
    pallas_call x1, Pallas kernels, on_device(): pl.pallas_call(functools.partial(kernel, (n_lon, n_lat, rows, cols)), out...  31.7 us
    unnamed x21, local copies, waits for them, and re-layouts  8.26 us

profile of v1, /device:TPU:0, one launch (start us, length us, event | category | flops | bytes accessed | tf_op | source)
XLA Modules:
  0.0 41.2 jit_solution(9234064232432948172)
XLA Ops:
  1.3 0.0 copy-start.8
  1.3 0.0 copy-start.7
  1.3 0.7 %copy-done.8 = f32[1024]{0:T(1024)S(1)} copy-done((f32[1024]{0:T(1024)S(1)}, f32[1024]{0:T(1024)}, u32[]{:S(2)}) %copy-start.8) | copy-done | bytes 4120
  2.0 0.0 copy-done.7
  2.0 0.0 copy-start
  2.0 0.9 %copy-done = f32[64,1024]{1,0:T(8,128)S(1)} copy-done((f32[64,1024]{1,0:T(8,128)S(1)}, f32[64,1024]{1,0:T(8,128)}, u32[]{:S(2)}) %copy-start) | copy-done | bytes 262168
  2.9 0.0 copy-start.1
  2.9 0.9 %copy-done.1 = f32[64,1024]{1,0:T(8,128)S(1)} copy-done((f32[64,1024]{1,0:T(8,128)S(1)}, f32[64,1024]{1,0:T(8,128)}, u32[]{:S(2)}) %copy-start.1) | copy-done | bytes 262168
  3.9 0.0 copy-start.2
  3.9 0.8 %copy-done.2 = s32[8192]{0:T(1024)S(1)} copy-done((s32[8192]{0:T(1024)S(1)}, s32[8192]{0:T(1024)}, u32[]{:S(2)}) %copy-start.2) | copy-done | bytes 32792
  4.6 0.0 copy-start.3
  4.6 0.8 %copy-done.3 = s32[8192]{0:T(1024)S(1)} copy-done((s32[8192]{0:T(1024)S(1)}, s32[8192]{0:T(1024)}, u32[]{:S(2)}) %copy-start.3) | copy-done | bytes 32792
  5.4 0.0 copy-start.4
  5.4 0.8 %copy-done.4 = s32[8192]{0:T(1024)S(1)} copy-done((s32[8192]{0:T(1024)S(1)}, s32[8192]{0:T(1024)}, u32[]{:S(2)}) %copy-start.4) | copy-done | bytes 32792
  6.2 0.0 copy-start.5
  6.2 0.8 %copy-done.5 = f32[8192]{0:T(1024)S(1)} copy-done((f32[8192]{0:T(1024)S(1)}, f32[8192]{0:T(1024)}, u32[]{:S(2)}) %copy-start.5) | copy-done | bytes 32792
  6.9 0.0 copy-start.6
  6.9 0.8 %copy-done.6 = f32[8192]{0:T(1024)S(1)} copy-done((f32[8192]{0:T(1024)S(1)}, f32[8192]{0:T(1024)}, u32[]{:S(2)}) %copy-start.6) | copy-done | bytes 32792
  7.7 31.7 %shard_map.121 = (f32[64,1024]{1,0:T(8,128)S(1)}, f32[8,128]{1,0:T(8,128)S(1)}, f32[8,128]{1,0:T(8,128)S(1)}) custom-call(f32[64,1024]{1,0:T(8,128)S(1)} %copy-done, f32[64,1024]{1,0:T(8,128)S(1)} %copy-done.1, s32[64,128]{1,0:T(8,128)S(1)} %bitcast.9, s32[64,128]{1,0:T(8,128)S(1)} %bitcast.10, s32[64,128]{1,0:T(8,128)S(1)} %bitcast.11, ...), custom_call_target="tpu_custom_call" | custom-call | tf_op jit(solution)/shard_map/pallas_call | solution.py:289
  39.3 0.7 %copy.17 = f32[64,1024]{1,0:T(8,128)} copy(f32[64,1024]{1,0:T(8,128)S(1)} %get-tuple-element.12) | data formatting | bytes 524288
  40.0 0.6 %copy.18 = f32[1024]{0:T(1024)} copy(f32[1024]{0:T(1024)S(1)} %bitcast.17) | data formatting | bytes 8192
  40.6 0.6 %copy.19 = f32[1024]{0:T(1024)} copy(f32[1024]{0:T(1024)S(1)} %bitcast.16) | data formatting | bytes 8192
Async XLA Ops:
  1.3 0.7 %copy-start.8 = (f32[1024]{0:T(1024)S(1)}, f32[1024]{0:T(1024)}, u32[]{:S(2)}) copy-start(f32[1024]{0:T(1024)} %param.19) | copy-start | bytes 12292
  1.3 0.7 %copy-start.7 = (f32[1024]{0:T(1024)S(1)}, f32[1024]{0:T(1024)}, u32[]{:S(2)}) copy-start(f32[1024]{0:T(1024)} %param.18) | copy-start | bytes 12292
  2.0 0.9 %copy-start = (f32[64,1024]{1,0:T(8,128)S(1)}, f32[64,1024]{1,0:T(8,128)}, u32[]{:S(2)}) copy-start(f32[64,1024]{1,0:T(8,128)} %bed_ref.1) | copy-start | bytes 786436
  2.9 0.9 %copy-start.1 = (f32[64,1024]{1,0:T(8,128)S(1)}, f32[64,1024]{1,0:T(8,128)}, u32[]{:S(2)}) copy-start(f32[64,1024]{1,0:T(8,128)} %cot_ref.1) | copy-start | bytes 786436
  3.9 0.8 %copy-start.2 = (s32[8192]{0:T(1024)S(1)}, s32[8192]{0:T(1024)}, u32[]{:S(2)}) copy-start(s32[8192]{0:T(1024)} %param.12) | copy-start | bytes 98308
  4.6 0.8 %copy-start.3 = (s32[8192]{0:T(1024)S(1)}, s32[8192]{0:T(1024)}, u32[]{:S(2)}) copy-start(s32[8192]{0:T(1024)} %param.13) | copy-start | bytes 98308
  5.4 0.8 %copy-start.4 = (s32[8192]{0:T(1024)S(1)}, s32[8192]{0:T(1024)}, u32[]{:S(2)}) copy-start(s32[8192]{0:T(1024)} %param.14) | copy-start | bytes 98308
  6.2 0.8 %copy-start.5 = (f32[8192]{0:T(1024)S(1)}, f32[8192]{0:T(1024)}, u32[]{:S(2)}) copy-start(f32[8192]{0:T(1024)} %param.15) | copy-start | bytes 98308
  6.9 0.8 %copy-start.6 = (f32[8192]{0:T(1024)S(1)}, f32[8192]{0:T(1024)}, u32[]{:S(2)}) copy-start(f32[8192]{0:T(1024)} %param.16) | copy-start | bytes 98308

commit v2 on v1

--- a/solution.py
+++ b/solution.py
@@ -27,21 +27,30 @@
     dims,
     bed_ref,
     cot_ref,
+    cell_in,
+    owner_in,
+    reach_in,
+    weight_in,
+    angle_in,
+    count_ref,
+    width_in,
+    rbed_in,
+    level_out,
+    gwidth_out,
+    gbed_out,
     cell_ref,
     owner_ref,
     reach_ref,
     weight_ref,
     angle_ref,
-    count_ref,
     width_ref,
     rbed_ref,
-    level_out,
-    gwidth_out,
-    gbed_out,
+    local_sem,
     bed,
     lev,
     fields,
     hot,
+    found,
     terms,
     spots,
     sums,
@@ -70,8 +79,24 @@
         return carry
 
     lax.fori_loop(1, owners, greet, 0)
-    lev[PAD_R : PAD_R + rows, PAD_C : PAD_C + cols] = cot_ref[...]
-    bed[PAD_R : PAD_R + rows, PAD_C : PAD_C + cols] = bed_ref[...]
+    middle = (pl.ds(PAD_R, rows), pl.ds(PAD_C, cols))
+    pairs = (
+        (weight_in, weight_ref),
+        (angle_in, angle_ref),
+        (bed_ref, bed.at[middle]),
+        (cot_ref, lev.at[middle]),
+        (cell_in, cell_ref),
+        (owner_in, owner_ref),
+        (reach_in, reach_ref),
+        (width_in, width_ref),
+        (rbed_in, rbed_ref),
+    )
+    loads = [
+        pltpu.make_async_copy(source, place, local_sem.at[i])
+        for i, (source, place) in enumerate(pairs)
+    ]
+    for load in loads:
+        load.start()
     pl.semaphore_wait(barrier, owners - 1)
 
     def span(step, length, pad):
@@ -102,6 +127,9 @@
             copy.start()
             copies.append(copy)
 
+    for load in loads:
+        load.wait()
+
     slot = (
         lax.broadcasted_iota(jnp.int32, (slot_rows, LANES), 0) * LANES
         + lax.broadcasted_iota(jnp.int32, (slot_rows, LANES), 1)
@@ -112,6 +140,32 @@
     weights[1] = weight * jnp.cos(angle)
     weights[2] = weight * jnp.sin(angle)
     sums[...] = jnp.zeros_like(sums)
+
+    half = cols // 2
+    picks = 2 * rows
+    reach_rows = width_ref.shape[0] // 2
+    per_owner = 2 * reach_rows
+    table = owners * per_owner
+    blocks = slot_rows // GROUP
+
+    def mark(number, carry):
+        here = pl.ds(pl.multiple_of(number * GROUP, GROUP), GROUP)
+        deep = cell_ref[here, :] % half
+        reach = reach_ref[here, :]
+        lane = (reach // LANES // reach_rows) * LANES + reach % LANES
+        deep_ids = lax.broadcasted_iota(jnp.int32, (half, LANES), 0)
+        lane_ids = lax.broadcasted_iota(jnp.int32, (TABLE, LANES), 0)
+        for i in range(GROUP):
+            at = slice(i * LANES, (i + 1) * LANES)
+            hot[number, :, at] = jnp.where(deep_ids == deep[i : i + 1], 1.0, 0.0).astype(
+                jnp.bfloat16
+            )
+            spots[number, :, at] = jnp.where(lane_ids == lane[i : i + 1], 1.0, 0.0).astype(
+                jnp.bfloat16
+            )
+        return carry
+
+    lax.fori_loop(0, blocks, mark, 0)
 
     for copy in copies:
         copy.wait()
@@ -159,8 +213,6 @@
             north_adj = north_keep * north_mid
     level_out[...] = level[PAD_R : PAD_R + rows, PAD_C : PAD_C + cols]
 
-    half = cols // 2
-    picks = 2 * rows
     for index, value in enumerate((sum_level, sum_east, sum_north)):
         for side in range(2):
             first = PAD_C + side * half
@@ -169,41 +221,28 @@
             fields[place, 0:half] = high.astype(jnp.bfloat16)
             fields[place, half : 2 * half] = low.astype(jnp.bfloat16)
 
-    reach_rows = width_ref.shape[0] // 2
-    per_owner = 2 * reach_rows
-    table = owners * per_owner
-    block = GROUP * LANES
-
-    def one_block(number, carry):
+    def found_in(number):
+        here = hot[number]
+        return jnp.dot(
+            fields[:, 0:half], here, preferred_element_type=jnp.float32
+        ) + jnp.dot(fields[:, half : 2 * half], here, preferred_element_type=jnp.float32)
+
+    def add_terms(number, side):
         here = pl.ds(pl.multiple_of(number * GROUP, GROUP), GROUP)
         cell = cell_ref[here, :]
-        column = cell % cols
-        deep = column % half
-        pick = (column // half) * rows + cell // cols
-        reach = reach_ref[here, :]
-        tile = reach // LANES
-        key = owner_ref[here, :] * reach_rows + tile % reach_rows
-        lane = (tile // reach_rows) * LANES + reach % LANES
+        pick = ((cell % cols) // half) * rows + cell // cols
+        key = owner_ref[here, :] * reach_rows + (reach_ref[here, :] // LANES) % reach_rows
         for_level, for_east, for_north = (weights[i, here, :] for i in range(3))
-        deep_ids = lax.broadcasted_iota(jnp.int32, (half, LANES), 0)
         pick_ids = lax.broadcasted_iota(jnp.int32, (picks, LANES), 0)
-        lane_ids = lax.broadcasted_iota(jnp.int32, (TABLE, LANES), 0)
         line_ids = lax.broadcasted_iota(jnp.int32, (table, LANES), 0)
         key_ids = (line_ids // per_owner) * reach_rows + line_ids % reach_rows
         is_flow = (line_ids // reach_rows) % 2 == 1
         for i in range(GROUP):
             at = slice(i * LANES, (i + 1) * LANES)
-            hot[:, at] = jnp.where(deep_ids == deep[i : i + 1], 1.0, 0.0).astype(jnp.bfloat16)
-            spots[:, at] = jnp.where(lane_ids == lane[i : i + 1], 1.0, 0.0).astype(jnp.bfloat16)
-        found = jnp.dot(
-            fields[:, 0:half], hot[...], preferred_element_type=jnp.float32
-        ) + jnp.dot(fields[:, half : 2 * half], hot[...], preferred_element_type=jnp.float32)
-        for i in range(GROUP):
-            at = slice(i * LANES, (i + 1) * LANES)
             mine = pick_ids == pick[i : i + 1]
             value = [
                 jnp.sum(
-                    jnp.where(mine, found[f * picks : (f + 1) * picks, at], 0.0),
+                    jnp.where(mine, found[side, f * picks : (f + 1) * picks, at], 0.0),
                     axis=0,
                     keepdims=True,
                 )
@@ -214,19 +253,32 @@
                 for_east[i : i + 1] * value[1] + for_north[i : i + 1] * value[2]
             )
             line = key_ids == key[i : i + 1]
-            terms[0:table, at] = jnp.where(
+            terms[side, 0:table, at] = jnp.where(
                 line, jnp.where(is_flow, flow_high, level_high), 0.0
             ).astype(jnp.bfloat16)
-            terms[table : 2 * table, at] = jnp.where(
+            terms[side, table : 2 * table, at] = jnp.where(
                 line, jnp.where(is_flow, flow_low, level_low), 0.0
             ).astype(jnp.bfloat16)
         added = lax.dot_general(
-            terms[...], spots[...], (((1,), (1,)), ((), ())), preferred_element_type=jnp.float32
+            terms[side],
+            spots[number],
+            (((1,), (1,)), ((), ())),
+            preferred_element_type=jnp.float32,
         )
         sums[...] += added[0:table] + added[table : 2 * table]
+
+    found[0] = found_in(0)
+
+    def two_blocks(pair, carry):
+        for side in range(2):
+            found[1 - side] = found_in(2 * pair + side + 1)
+            add_terms(2 * pair + side, side)
         return carry
 
-    lax.fori_loop(0, slot_rows * LANES // block, one_block, 0)
+    lax.fori_loop(0, blocks // 2 - 1, two_blocks, 0)
+    found[1] = found_in(blocks - 1)
+    add_terms(blocks - 2, 0)
+    add_terms(blocks - 1, 1)
 
     def outgoing(step):
         other = lax.rem(me + step, owners)
@@ -281,10 +333,12 @@
     reach_tiles = reach_width.shape[0] // LANES
     per_owner = reach_tiles
     block = GROUP * LANES
+    blocks = slot_rows // GROUP
 
     def tiled(value):
         return value.reshape(-1, LANES)
 
+    hbm = pl.BlockSpec(memory_space=pltpu.HBM)
     vmem = pl.BlockSpec(memory_space=pltpu.VMEM)
     level, gwidth, gbed = pl.pallas_call(
         functools.partial(kernel, (n_lon, n_lat, rows, cols)),
@@ -293,15 +347,24 @@
             jax.ShapeDtypeStruct((reach_tiles, LANES), jnp.float32),
             jax.ShapeDtypeStruct((reach_tiles, LANES), jnp.float32),
         ),
-        in_specs=[vmem] * 7 + [pl.BlockSpec(memory_space=pltpu.SMEM)] + [vmem] * 2,
+        in_specs=[hbm] * 7 + [pl.BlockSpec(memory_space=pltpu.SMEM)] + [hbm] * 2,
         out_specs=(vmem, vmem, vmem),
         scratch_shapes=[
+            pltpu.VMEM((slot_rows, LANES), jnp.int32),
+            pltpu.VMEM((slot_rows, LANES), jnp.int32),
+            pltpu.VMEM((slot_rows, LANES), jnp.int32),
+            pltpu.VMEM((slot_rows, LANES), jnp.float32),
+            pltpu.VMEM((slot_rows, LANES), jnp.float32),
+            pltpu.VMEM((reach_tiles, LANES), jnp.float32),
+            pltpu.VMEM((reach_tiles, LANES), jnp.float32),
+            pltpu.SemaphoreType.DMA((9,)),
             pltpu.VMEM((tall, wide), jnp.float32),
             pltpu.VMEM((tall, wide), jnp.float32),
             pltpu.VMEM((6 * rows, cols), jnp.bfloat16),
-            pltpu.VMEM((cols // 2, block), jnp.bfloat16),
-            pltpu.VMEM((2 * owners * per_owner, block), jnp.bfloat16),
-            pltpu.VMEM((TABLE, block), jnp.bfloat16),
+            pltpu.VMEM((blocks, cols // 2, block), jnp.bfloat16),
+            pltpu.VMEM((2, 6 * rows, block), jnp.float32),
+            pltpu.VMEM((2, 2 * owners * per_owner, block), jnp.bfloat16),
+            pltpu.VMEM((blocks, TABLE, block), jnp.bfloat16),
             pltpu.VMEM((owners * per_owner, TABLE), jnp.float32),
             pltpu.VMEM((owners, per_owner, TABLE), jnp.float32),
             pltpu.VMEM((3, slot_rows, LANES), jnp.float32),
@@ -311,7 +374,7 @@
             pltpu.SemaphoreType.DMA((owners,)),
         ],
         compiler_params=pltpu.CompilerParams(
-            collective_id=0, has_side_effects=True, vmem_limit_bytes=48 << 20
+            collective_id=0, has_side_effects=True, vmem_limit_bytes=63 << 20
         ),
     )(
         bed_depth,

time: 41.8 us -> 33.8 us (0.81)
  local copies, waits for them, and re-layouts: 8.26 us -> 2.95 us
  Pallas kernels: 31.7 us -> 29.4 us
    unnamed x21 -> x7, local copies, waits for them, and re-layouts: 8.26 us -> 2.95 us
    pallas_call x1, Pallas kernels: 31.7 us -> 29.4 us  [on_device(): pl.pallas_call(functools.partial(kernel, (n_lon, n_lat, rows, cols)), out...]
where the time goes in v2:
time: 33.8 us; the launch traced here: 33.6 us
  Pallas kernels  29.4 us (87%)
  local copies, waits for them, and re-layouts  2.95 us (9%)
  between operations  1.3 us (4%)
    pallas_call x1, Pallas kernels, on_device(): pl.pallas_call(functools.partial(kernel, (n_lon, n_lat, rows, cols)), out...  29.4 us
    unnamed x7, local copies, waits for them, and re-layouts  2.95 us

profile of v2, /device:TPU:0, one launch (start us, length us, event | category | flops | bytes accessed | tf_op | source)
XLA Modules:
  0.0 33.6 jit_solution(9889838900855675867)
XLA Ops:
  1.3 29.4 %shard_map.121 = (f32[64,1024]{1,0:T(8,128)}, f32[8,128]{1,0:T(8,128)}, f32[8,128]{1,0:T(8,128)}) custom-call(f32[64,1024]{1,0:T(8,128)} %bed_ref.1, f32[64,1024]{1,0:T(8,128)} %cot_ref.1, s32[64,128]{1,0:T(8,128)} %bitcast.9, s32[64,128]{1,0:T(8,128)} %bitcast.10, s32[64,128]{1,0:T(8,128)} %bitcast.11, f32[64,128]{1,0:T(8,128)} %bitcast.12, ...), custom_call_target="tpu_custom_call" | custom-call | tf_op jit(solution)/shard_map/pallas_call | solution.py:343
  30.7 0.0 copy-start.1
  30.7 1.7 %copy.17 = f32[64,1024]{1,0:T(8,128)} copy(f32[64,1024]{1,0:T(8,128)} %get-tuple-element.12) | data formatting | bytes 524288
  32.4 0.0 copy-done.1
  32.4 0.0 copy-start
  32.4 0.6 %copy.18 = f32[1024]{0:T(1024)} copy(f32[1024]{0:T(1024)S(1)} %bitcast.17) | data formatting | bytes 8192
  33.0 0.1 copy-done
  33.0 0.6 %copy.19 = f32[1024]{0:T(1024)} copy(f32[1024]{0:T(1024)S(1)} %bitcast.16) | data formatting | bytes 8192
Async XLA Ops:
  30.7 1.7 %copy-start.1 = (f32[8,128]{1,0:T(8,128)S(1)}, f32[8,128]{1,0:T(8,128)}, u32[]{:S(2)}) copy-start(f32[8,128]{1,0:T(8,128)} %get-tuple-element.7) | copy-start | bytes 12292
  32.4 0.7 %copy-start = (f32[8,128]{1,0:T(8,128)S(1)}, f32[8,128]{1,0:T(8,128)}, u32[]{:S(2)}) copy-start(f32[8,128]{1,0:T(8,128)} %get-tuple-element.8) | copy-start | bytes 12292

commit v3 on v2

--- a/solution.py
+++ b/solution.py
@@ -339,6 +339,9 @@
         return value.reshape(-1, LANES)
 
     hbm = pl.BlockSpec(memory_space=pltpu.HBM)
+    def in_hbm(value):
+        return pltpu.with_memory_space_constraint(value, pltpu.HBM)
+
     vmem = pl.BlockSpec(memory_space=pltpu.VMEM)
     level, gwidth, gbed = pl.pallas_call(
         functools.partial(kernel, (n_lon, n_lat, rows, cols)),
@@ -374,19 +377,19 @@
             pltpu.SemaphoreType.DMA((owners,)),
         ],
         compiler_params=pltpu.CompilerParams(
-            collective_id=0, has_side_effects=True, vmem_limit_bytes=63 << 20
+            collective_id=0, has_side_effects=True, vmem_limit_bytes=48 << 20
         ),
     )(
-        bed_depth,
-        cotangent,
-        tiled(sample_cell),
-        tiled(sample_owner),
-        tiled(sample_reach),
-        tiled(sample_weight),
-        tiled(sample_angle),
+        in_hbm(bed_depth),
+        in_hbm(cotangent),
+        in_hbm(tiled(sample_cell)),
+        in_hbm(tiled(sample_owner)),
+        in_hbm(tiled(sample_reach)),
+        in_hbm(tiled(sample_weight)),
+        in_hbm(tiled(sample_angle)),
         sample_count,
-        tiled(reach_width),
-        tiled(reach_bed),
+        in_hbm(tiled(reach_width)),
+        in_hbm(tiled(reach_bed)),
     )
     return level, gwidth.reshape(-1), gbed.reshape(-1)
 

time: 33.8 us -> 32 us (0.947)
  local copies, waits for them, and re-layouts: 2.95 us -> 1.89 us
  Pallas kernels: 29.4 us -> 28.7 us
    unnamed x7 -> x3, local copies, waits for them, and re-layouts: 2.95 us -> 1.89 us
    pallas_call x1, Pallas kernels: 29.4 us -> 28.7 us  [on_device(): pl.pallas_call(functools.partial(kernel, (n_lon, n_lat, rows, cols)), out...]
where the time goes in v3:
time: 32 us; the launch traced here: 31.9 us
  Pallas kernels  28.7 us (90%)
  local copies, waits for them, and re-layouts  1.89 us (6%)
  between operations  1.29 us (4%)
    pallas_call x1, Pallas kernels, on_device(): pl.pallas_call(functools.partial(kernel, (n_lon, n_lat, rows, cols)), out...  28.7 us
    unnamed x3, local copies, waits for them, and re-layouts  1.89 us

profile of v3, /device:TPU:0, one launch (start us, length us, event | category | flops | bytes accessed | tf_op | source)
XLA Modules:
  0.0 31.9 jit_solution(17324243876089975270)
XLA Ops:
  1.3 28.7 %shard_map.121 = (f32[64,1024]{1,0:T(8,128)S(1)}, f32[8,128]{1,0:T(8,128)S(1)}, f32[8,128]{1,0:T(8,128)S(1)}) custom-call(f32[64,1024]{1,0:T(8,128)} %bed_ref.1, f32[64,1024]{1,0:T(8,128)} %cot_ref.1, s32[64,128]{1,0:T(8,128)} %bitcast.11, s32[64,128]{1,0:T(8,128)} %bitcast.12, s32[64,128]{1,0:T(8,128)} %bitcast.13, f32[64,128]{1,0:T(8,128)} %bitcast.14, ...), custom_call_target="tpu_custom_call" | custom-call | tf_op jit(solution)/shard_map/pallas_call | solution.py:346
  30.0 0.7 %copy.17 = f32[64,1024]{1,0:T(8,128)} copy(f32[64,1024]{1,0:T(8,128)S(1)} %get-tuple-element.12) | data formatting | bytes 524288
  30.7 0.6 %copy.18 = f32[1024]{0:T(1024)} copy(f32[1024]{0:T(1024)S(1)} %bitcast.10) | data formatting | bytes 8192
  31.3 0.6 %copy.19 = f32[1024]{0:T(1024)} copy(f32[1024]{0:T(1024)S(1)} %bitcast.9) | data formatting | bytes 8192

commit v4 on v3

--- a/solution.py
+++ b/solution.py
@@ -78,7 +78,7 @@
         pl.semaphore_signal(barrier, inc=1, device_id=peer(step), device_id_type=MESH)
         return carry
 
-    lax.fori_loop(1, owners, greet, 0)
+    lax.fori_loop(1, owners, greet, 0, unroll=5)
     middle = (pl.ds(PAD_R, rows), pl.ds(PAD_C, cols))
     pairs = (
         (weight_in, weight_ref),
@@ -97,6 +97,25 @@
     ]
     for load in loads:
         load.start()
+    half = cols // 2
+    picks = 2 * rows
+    reach_rows = width_ref.shape[0] // 2
+    per_owner = 2 * reach_rows
+    table = owners * per_owner
+    blocks = slot_rows // GROUP
+
+    def mark_reach(number, carry):
+        here = pl.ds(pl.multiple_of(number * GROUP, GROUP), GROUP)
+        reach = reach_ref[here, :]
+        lane = (reach // LANES // reach_rows) * LANES + reach % LANES
+        upright = jnp.transpose(lane.astype(jnp.float32)).astype(jnp.int32)
+        lane_ids = lax.broadcasted_iota(jnp.int32, (LANES, TABLE), 1)
+        for i in range(GROUP):
+            spots[number, i * LANES : (i + 1) * LANES, :] = jnp.where(
+                lane_ids == upright[:, i : i + 1], 1.0, 0.0
+            ).astype(jnp.bfloat16)
+        return carry
+
     pl.semaphore_wait(barrier, owners - 1)
 
     def span(step, length, pad):
@@ -129,6 +148,7 @@
 
     for load in loads:
         load.wait()
+    lax.fori_loop(0, blocks, mark_reach, 0)
 
     slot = (
         lax.broadcasted_iota(jnp.int32, (slot_rows, LANES), 0) * LANES
@@ -141,26 +161,13 @@
     weights[2] = weight * jnp.sin(angle)
     sums[...] = jnp.zeros_like(sums)
 
-    half = cols // 2
-    picks = 2 * rows
-    reach_rows = width_ref.shape[0] // 2
-    per_owner = 2 * reach_rows
-    table = owners * per_owner
-    blocks = slot_rows // GROUP
-
     def mark(number, carry):
         here = pl.ds(pl.multiple_of(number * GROUP, GROUP), GROUP)
         deep = cell_ref[here, :] % half
-        reach = reach_ref[here, :]
-        lane = (reach // LANES // reach_rows) * LANES + reach % LANES
         deep_ids = lax.broadcasted_iota(jnp.int32, (half, LANES), 0)
-        lane_ids = lax.broadcasted_iota(jnp.int32, (TABLE, LANES), 0)
         for i in range(GROUP):
             at = slice(i * LANES, (i + 1) * LANES)
             hot[number, :, at] = jnp.where(deep_ids == deep[i : i + 1], 1.0, 0.0).astype(
-                jnp.bfloat16
-            )
-            spots[number, :, at] = jnp.where(lane_ids == lane[i : i + 1], 1.0, 0.0).astype(
                 jnp.bfloat16
             )
         return carry
@@ -259,12 +266,7 @@
             terms[side, table : 2 * table, at] = jnp.where(
                 line, jnp.where(is_flow, flow_low, level_low), 0.0
             ).astype(jnp.bfloat16)
-        added = lax.dot_general(
-            terms[side],
-            spots[number],
-            (((1,), (1,)), ((), ())),
-            preferred_element_type=jnp.float32,
-        )
+        added = jnp.dot(terms[side], spots[number], preferred_element_type=jnp.float32)
         sums[...] += added[0:table] + added[table : 2 * table]
 
     found[0] = found_in(0)
@@ -299,9 +301,9 @@
         outgoing(step).wait()
         return total + recv[step]
 
-    lax.fori_loop(1, owners, send, 0)
+    lax.fori_loop(1, owners, send, 0, unroll=5)
     own = sums[pl.ds(pl.multiple_of(me * per_owner, per_owner), per_owner), :]
-    total = lax.fori_loop(1, owners, take, own)
+    total = lax.fori_loop(1, owners, take, own, unroll=5)
     level_total = jnp.concatenate(
         [total[0:reach_rows, 0:LANES], total[0:reach_rows, LANES:TABLE]], axis=0
     )
@@ -367,7 +369,7 @@
             pltpu.VMEM((blocks, cols // 2, block), jnp.bfloat16),
             pltpu.VMEM((2, 6 * rows, block), jnp.float32),
             pltpu.VMEM((2, 2 * owners * per_owner, block), jnp.bfloat16),
-            pltpu.VMEM((blocks, TABLE, block), jnp.bfloat16),
+            pltpu.VMEM((blocks, block, TABLE), jnp.bfloat16),
             pltpu.VMEM((owners * per_owner, TABLE), jnp.float32),
             pltpu.VMEM((owners, per_owner, TABLE), jnp.float32),
             pltpu.VMEM((3, slot_rows, LANES), jnp.float32),

time: 32 us -> 31.9 us (level)
  no operation moved by 1% of the time
where the time goes in v4:
time: 31.9 us; the launch traced here: 31.8 us
  Pallas kernels  28.6 us (90%)
  local copies, waits for them, and re-layouts  1.89 us (6%)
  between operations  1.29 us (4%)
    pallas_call x1, Pallas kernels, on_device(): pl.pallas_call(functools.partial(kernel, (n_lon, n_lat, rows, cols)), out...  28.6 us
    unnamed x3, local copies, waits for them, and re-layouts  1.89 us

profile of v4, /device:TPU:0, one launch (start us, length us, event | category | flops | bytes accessed | tf_op | source)
XLA Modules:
  0.0 31.8 jit_solution(17944135458986308918)
XLA Ops:
  1.3 28.6 %shard_map.121 = (f32[64,1024]{1,0:T(8,128)S(1)}, f32[8,128]{1,0:T(8,128)S(1)}, f32[8,128]{1,0:T(8,128)S(1)}) custom-call(f32[64,1024]{1,0:T(8,128)} %bed_ref.1, f32[64,1024]{1,0:T(8,128)} %cot_ref.1, s32[64,128]{1,0:T(8,128)} %bitcast.11, s32[64,128]{1,0:T(8,128)} %bitcast.12, s32[64,128]{1,0:T(8,128)} %bitcast.13, f32[64,128]{1,0:T(8,128)} %bitcast.14, ...), custom_call_target="tpu_custom_call" | custom-call | tf_op jit(solution)/shard_map/pallas_call | solution.py:348
  29.9 0.7 %copy.17 = f32[64,1024]{1,0:T(8,128)} copy(f32[64,1024]{1,0:T(8,128)S(1)} %get-tuple-element.12) | data formatting | bytes 524288
  30.6 0.6 %copy.18 = f32[1024]{0:T(1024)} copy(f32[1024]{0:T(1024)S(1)} %bitcast.10) | data formatting | bytes 8192
  31.2 0.6 %copy.19 = f32[1024]{0:T(1024)} copy(f32[1024]{0:T(1024)S(1)} %bitcast.9) | data formatting | bytes 8192
